TPU v7x, 32 devices: a whole 2x2x4 slice. The times are simulated.
32 devices in a mesh: feat: 16 (over z, y, core), width: 2 (over x).
Axes of the slice: x: 2, y: 2, z: 4, core: 2. Of those that a mesh axis runs over, the one named last changes fastest.
Arguments:
- residual: bfloat16 [2, 448, 3584], P(None, None, 'width'), may hold values from -6 to 6
- targets: bfloat16 [2, 448, 3584], P(None, None, 'width'), may hold values from -6 to 6
- encoder: bfloat16 [3584, 32768], P('width', 'feat'), may hold values from -0.09375 to 0.09375
- biases: bfloat16 [32768], P('feat'), may hold values from -3 to 3
- same_decoder: bfloat16 [32768, 3584], P('feat', 'width'), may hold values from -0.03125 to 0.03125
- next_decoder: bfloat16 [16384, 3584], P('feat', 'width'), may hold values from -0.03125 to 0.03125
- encoder_first: bfloat16 [3584, 32768], P('width', 'feat'), may hold values from -24 to 24
- encoder_second: bfloat16 [3584, 32768], P('width', 'feat'), may hold values from 4 to 64
- biases_first: bfloat16 [32768], P('feat'), may hold values from -24 to 24
- biases_second: bfloat16 [32768], P('feat'), may hold values from 4 to 64
- same_first: bfloat16 [32768, 3584], P('feat', 'width'), may hold values from -24 to 24
- same_second: bfloat16 [32768, 3584], P('feat', 'width'), may hold values from 4 to 64
- next_first: bfloat16 [16384, 3584], P('feat', 'width'), may hold values from -24 to 24
- next_second: bfloat16 [16384, 3584], P('feat', 'width'), may hold values from 4 to 64
Outputs:
- updated_encoder: bfloat16 [3584, 32768], P('width', 'feat')
- updated_biases: bfloat16 [32768], P('feat')
- updated_same: bfloat16 [32768, 3584], P('feat', 'width')
- updated_next: bfloat16 [16384, 3584], P('feat', 'width')
- encoder_moment: bfloat16 [3584, 32768], P('width', 'feat')
- encoder_square: bfloat16 [3584, 32768], P('width', 'feat')
- biases_moment: bfloat16 [32768], P('feat')
- biases_square: bfloat16 [32768], P('feat')
- same_moment: bfloat16 [32768, 3584], P('feat', 'width')
- same_square: bfloat16 [32768, 3584], P('feat', 'width')
- next_moment: bfloat16 [16384, 3584], P('feat', 'width')
- next_square: bfloat16 [16384, 3584], P('feat', 'width')
All inputs are finite; a program needn't handle non-finite values.
Results may differ from a plain program's by a relative error of at most 0.0055.
Values may be sent and summed in bfloat16 or wider, within the bound.
No kernel may reach another device: no remote copies, remote signals or barrier semaphores. Data moves between devices by JAX's collectives and lax.ppermute only.
A program may use at most 256 MiB of HBM per device.

v0:
```python
import jax
import jax.numpy as jnp
from jax import lax
from jax.sharding import PartitionSpec as P

STEPS = 100


beta_one = 0.9
beta_two = 0.999
learn_rate = 0.002
adam_eps = 1e-08
weight_decay = 0.1


def shifted(value, axis, steps):
    count = lax.axis_size(axis)
    leading, last = (max(0, -steps), min(count, count - steps))
    return lax.ppermute(value, axis, [(source, source + steps) for source in range(leading, last)])


def adamw_update(parameter, first, second, gradient, decay_rate):
    first_new = beta_one * first.astype(jnp.float32) + (1.0 - beta_one) * gradient
    second_new = beta_two * second.astype(jnp.float32) + (1.0 - beta_two) * gradient * gradient
    first_hat = first_new / (1.0 - beta_one**STEPS)
    second_hat = second_new / (1.0 - beta_two**STEPS)
    weight = parameter.astype(jnp.float32)
    updated = weight - learn_rate * (
        first_hat / (jnp.sqrt(second_hat) + adam_eps) + decay_rate * weight
    )
    return (
        updated.astype(jnp.bfloat16),
        first_new.astype(jnp.bfloat16),
        second_new.astype(jnp.bfloat16),
    )


def over_rows(left, right):
    return lax.dot_general(
        left, right, (((0,), (0,)), ((), ())), preferred_element_type=jnp.float32
    )


def over_cols(left, right):
    return lax.dot_general(
        left, right, (((1,), (1,)), ((), ())), preferred_element_type=jnp.float32
    )


def local(
    residual,
    targets,
    encoder,
    biases,
    same_decoder,
    next_decoder,
    encoder_first,
    encoder_second,
    biases_first,
    biases_second,
    same_first,
    same_second,
    next_first,
    next_second,
):
    feat_count = lax.axis_size("feat")
    feat_index = lax.axis_index("feat")
    layers_total = residual.shape[0]
    per_layer = feat_count // layers_total
    source_layer = feat_index // per_layer
    leading = source_layer == 0
    half_count = feat_count // 2
    half_width = encoder.shape[1] // 2
    inputs_local = lax.dynamic_index_in_dim(residual, source_layer, 0, keepdims=False)
    partial_pre = jnp.dot(inputs_local, encoder, preferred_element_type=jnp.float32)
    preact = lax.psum(partial_pre, "width") + biases.astype(jnp.float32)
    active = jnp.maximum(preact, 0.0).astype(jnp.bfloat16)
    received = shifted(active[:, half_width:], "feat", half_count)
    cross_input = jnp.where(leading, active[:, :half_width], received)
    own_term = jnp.dot(active, same_decoder, preferred_element_type=jnp.float32)
    cross_term = jnp.dot(cross_input, next_decoder, preferred_element_type=jnp.float32)
    first_target = jnp.where(leading, own_term, jnp.zeros_like(own_term))
    second_target = jnp.where(leading, cross_term, own_term + cross_term)
    partial_recon = jnp.stack([first_target, second_target])
    recon_total = lax.psum(partial_recon, "feat")
    delta = (recon_total - targets.astype(jnp.float32)).astype(jnp.bfloat16)
    delta_own = lax.dynamic_index_in_dim(delta, source_layer, 0, keepdims=False)
    delta_next = delta[1]
    grad_same = over_rows(active, delta_own)
    grad_next = over_rows(cross_input, delta_next)
    own_back = over_cols(delta_own, same_decoder)
    cross_back = over_cols(delta_next, next_decoder)
    returned = shifted(cross_back.astype(jnp.bfloat16), "feat", -half_count).astype(
        cross_back.dtype
    )
    returned_sum = jnp.where(
        leading, jnp.concatenate([cross_back, returned], axis=1), jnp.zeros_like(own_back)
    )
    feature_grad = lax.psum((own_back + returned_sum).astype(jnp.bfloat16), "width").astype(
        jnp.float32
    )
    preact_grad = jnp.where(preact > 0.0, feature_grad, 0.0)
    grad_biases = jnp.sum(preact_grad, axis=0)
    grad_encoder = over_rows(inputs_local, preact_grad.astype(jnp.bfloat16))
    updated_encoder, encoder_moment, encoder_square = adamw_update(
        encoder, encoder_first, encoder_second, grad_encoder, weight_decay
    )
    updated_biases, biases_moment, biases_square = adamw_update(
        biases, biases_first, biases_second, grad_biases, 0.0
    )
    updated_same, same_moment, same_square = adamw_update(
        same_decoder, same_first, same_second, grad_same, weight_decay
    )
    updated_next, next_moment, next_square = adamw_update(
        next_decoder, next_first, next_second, grad_next, weight_decay
    )
    return (
        updated_encoder,
        updated_biases,
        updated_same,
        updated_next,
        encoder_moment,
        encoder_square,
        biases_moment,
        biases_square,
        same_moment,
        same_square,
        next_moment,
        next_square,
    )


def solution(mesh):
    in_specs = (
        P(None, None, "width"),
        P(None, None, "width"),
        P("width", "feat"),
        P("feat"),
        P("feat", "width"),
        P("feat", "width"),
        P("width", "feat"),
        P("width", "feat"),
        P("feat"),
        P("feat"),
        P("feat", "width"),
        P("feat", "width"),
        P("feat", "width"),
        P("feat", "width"),
    )
    out_specs = (
        P("width", "feat"),
        P("feat"),
        P("feat", "width"),
        P("feat", "width"),
        P("width", "feat"),
        P("width", "feat"),
        P("feat"),
        P("feat"),
        P("feat", "width"),
        P("feat", "width"),
        P("feat", "width"),
        P("feat", "width"),
    )
    return jax.shard_map(local, mesh=mesh, in_specs=in_specs, out_specs=out_specs, check_vma=False)
```

profile of v0, /device:TPU:20, one launch (start us, length us, event | category | flops | bytes accessed | tf_op | source)
XLA Modules:
  0.0 470.3 jit_solution(2566604312762460103)
XLA Ops:
  7.2 0.0 copy-start
  7.2 0.0 all-reduce.4.cloned.1.call-start
  7.3 1.8 copy-done
  9.1 0.0 copy-start.3
  9.1 8.4 %fusion.33 = f32[448,2048]{1,0:T(8,128)} fusion(bf16[1792,2048]{1,0:T(8,128)(2,1)} %param.16, bf16[2,448,1792]{2,1,0:T(8,128)(2,1)S(1)} %copy-done, s32[]{:T(128)S(6)} %select_n.43), kind=kOutput, calls=%fused_computation.51 | convolution fusion | flops 3288334336 | bytes 12615684 | tf_op jit(solution)/shard_map/dot_general | solution.py:75
  17.5 0.0 all-reduce.4.cloned.1.call-update
  17.5 0.0 all-reduce.6.cloned.1.call-start
  17.6 0.0 copy-done.3
  17.6 98.3 %all-reduce.4.cloned.1.call-done = f32[448,2048]{1,0:T(8,128)} async-done(((f32[448,2048]{1,0:T(8,128)}), f32[448,2048]{1,0:T(8,128)}) %all-reduce.4.cloned.1.call-update) | async-done | bytes 3670032 | tf_op jit(solution)/shard_map/psum | solution.py:76
  115.9 2.5 maximum_convert_fusion
  118.4 0.0 copy-start.1
  118.4 0.1 slice.13
  118.5 0.0 copy-start.6
  118.5 1.6 collective-permute-start
  120.1 6.7 %fusion.51 = f32[448,1792]{1,0:T(8,128)S(1)} fusion(bf16[448,2048]{1,0:T(8,128)(2,1)S(1)} %maximum_convert_fusion, bf16[2048,1792]{1,0:T(8,128)(2,1)} %param.18), kind=kOutput, calls=%fused_computation.73 | convolution fusion | flops 3288334336 | bytes 12386304 | tf_op jit(solution)/shard_map/dot_general | solution.py:80
  126.7 0.2 select_bitcast_fusion
  127.0 16.8 %collective-permute-done = bf16[448,1024]{1,0:T(8,128)(2,1)S(1)} collective-permute-done((bf16[448,1024]{1,0:T(8,128)(2,1)S(1)}, bf16[448,1024]{1,0:T(8,128)(2,1)S(1)}, u32[]{:S(2)}, u32[]{:S(2)}) %collective-permute-start) | collective-permute-done | bytes 917536 | tf_op jit(solution)/shard_map/ppermute | solution.py:19
  143.7 0.0 copy-done.1
  143.7 0.0 copy-start.8
  143.7 0.9 copy-done.8
  144.7 0.0 copy-done.6
  144.7 1.9 fusion.22
  146.6 3.2 pad_maximum_fusion
  149.7 0.0 all-reduce.6.cloned.1.call-update
  149.8 0.0 all-reduce.8.cloned.1.call-start
  149.8 161.1 %all-reduce.6.cloned.1.call-done = f32[2,448,1792]{2,1,0:T(8,128)} async-done(((f32[2,448,1792]{2,1,0:T(8,128)}), f32[2,448,1792]{2,1,0:T(8,128)}) %all-reduce.6.cloned.1.call-update) | async-done | bytes 6422544 | tf_op jit(solution)/shard_map/psum | solution.py:85
  310.9 0.0 copy-start.7
  310.9 4.6 subtract_convert_fusion
  315.5 0.0 copy-start.2
  315.5 1.7 copy-done.2
  317.2 0.0 copy-done.7
  317.2 3.4 fusion.50
  320.6 3.6 collective-permute-start.1
  324.2 27.0 %fusion.10 = (bf16[2048,1792]{1,0:T(8,128)(2,1)}, bf16[2048,1792]{1,0:T(8,128)(2,1)}, bf16[2048,1792]{1,0:T(8,128)(2,1)}) fusion(bf16[2048,1792]{1,0:T(8,128)(2,1)} %param.25, bf16[2048,1792]{1,0:T(8,128)(2,1)} %param.24, bf16[2048,1792]{1,0:T(8,128)(2,1)} %param.18, bf16[448,2048]{1,0:T(8,128)(2,1)} %copy-done.1, bf16[2,448,1792]{2,1,0:T(8,128)(2,1)} %copy-done.2, ...), kind=kOutput, calls=%fused_computation.21 | convolution fusion | flops 3365404672 | bytes 47480836 | tf_op jit(solution)/shard_map/dot_general | solution.py:39
  351.2 11.8 %collective-permute-done.1 = bf16[448,1024]{1,0:T(8,128)(2,1)} collective-permute-done((bf16[448,1024]{1,0:T(8,128)(2,1)}, bf16[448,1024]{1,0:T(8,128)(2,1)}, u32[]{:S(2)}, u32[]{:S(2)}) %collective-permute-start.1) | collective-permute-done | bytes 917536 | tf_op jit(solution)/shard_map/ppermute | solution.py:19
  363.0 1.4 convert_element_type.104
  364.3 8.8 %fusion.19 = bf16[448,2048]{1,0:T(8,128)(2,1)} fusion(f32[448,1024]{1,0:T(8,128)S(1)} %convert_element_type.104, f32[448,1024]{1,0:T(8,128)} %get-tuple-element.27, pred[]{:T(512)S(6)} %eq.3, bf16[2048,1792]{1,0:T(8,128)(2,1)} %param.18, bf16[2,448,1792]{2,1,0:T(8,128)(2,1)} %copy-done.2, s32[]{:T(128)S(6)} %select_n.43), kind=kOutput, calls=%fused_computation.35 | convolution fusion | flops 3292004352 | bytes 14450693 | tf_op jit(solution)/shard_map/dot_general | solution.py:45
  373.2 0.0 all-reduce.8.cloned.1.call-update
  373.2 0.0 copy-start.4
  373.2 0.0 copy-start.5
  373.2 14.7 %fusion.17 = (bf16[1024,1792]{1,0:T(8,128)(2,1)}, bf16[1024,1792]{1,0:T(8,128)(2,1)}, bf16[1024,1792]{1,0:T(8,128)(2,1)}) fusion(bf16[1024,1792]{1,0:T(8,128)(2,1)} %param.27, bf16[1024,1792]{1,0:T(8,128)(2,1)} %param.26, bf16[1024,1792]{1,0:T(8,128)(2,1)} %param.19, bf16[2,448,1792]{2,1,0:T(8,128)(2,1)} %copy-done.2, bf16[448,1024]{1,0:T(8,128)(2,1)} %copy-done.8, ...), kind=kOutput, calls=%fused_computation.32 | convolution fusion | flops 1683161088 | bytes 25460736 | tf_op jit(solution)/shard_map/dot_general | solution.py:39
  388.0 43.6 %all-reduce.8.cloned.1.call-done = bf16[448,2048]{1,0:T(8,128)(2,1)} async-done(((bf16[448,2048]{1,0:T(8,128)(2,1)}), bf16[448,2048]{1,0:T(8,128)(2,1)}) %all-reduce.8.cloned.1.call-update) | async-done | bytes 1835024 | tf_op jit(solution)/shard_map/psum | solution.py:99
  431.5 4.5 fusion.20
  436.0 0.0 copy-done.4
  436.0 0.0 copy-done.5
  436.0 0.6 fusion.44
  436.7 27.1 %fusion.11 = (bf16[1792,2048]{1,0:T(8,128)(2,1)}, bf16[1792,2048]{1,0:T(8,128)(2,1)}, bf16[1792,2048]{1,0:T(8,128)(2,1)}) fusion(bf16[1792,2048]{1,0:T(8,128)(2,1)} %param.21, bf16[1792,2048]{1,0:T(8,128)(2,1)} %param.20, bf16[1792,2048]{1,0:T(8,128)(2,1)} %param.16, pred[448,2048]{1,0:T(32,128)(4,1)} %get-tuple-element.13, ...), kind=kOutput, calls=%fused_computation.22 | convolution fusion | flops 3368157184 | bytes 48398340 | tf_op jit(solution)/shard_map/dot_general | solution.py:39
  (1 shorter events, 0.0 us)
Async XLA Ops:
  7.2 1.9 copy-start
  7.2 108.7 %all-reduce.4.cloned.1.call-start = ((), (), s32[]{:S(2)}) async-start(), calls=%async_computation | async-start | bytes 7340032 | tf_op jit(solution)/shard_map/psum | solution.py:76
  9.1 8.5 %copy-start.3 = (bf16[2048]{0:T(1024)(128)(2,1)S(1)}, bf16[2048]{0:T(1024)(128)(2,1)}, u32[]{:S(2)}) copy-start(bf16[2048]{0:T(1024)(128)(2,1)} %param.17) | copy-start | bytes 12292
  17.5 293.4 %all-reduce.6.cloned.1.call-start = ((), (), s32[]{:S(2)}) async-start(), calls=%async_computation.1 | async-start | bytes 12845056 | tf_op jit(solution)/shard_map/psum | solution.py:85
  118.4 25.4 %copy-start.1 = (bf16[448,2048]{1,0:T(8,128)(2,1)}, bf16[448,2048]{1,0:T(8,128)(2,1)S(1)}, u32[]{:S(2)}) copy-start(bf16[448,2048]{1,0:T(8,128)(2,1)S(1)} %maximum_convert_fusion) | copy-start | bytes 5505028
  118.5 26.2 %copy-start.6 = (bf16[1024,1792]{1,0:T(8,128)(2,1)S(1)}, bf16[1024,1792]{1,0:T(8,128)(2,1)}, u32[]{:S(2)}) copy-start(bf16[1024,1792]{1,0:T(8,128)(2,1)} %param.19) | copy-start | bytes 11010052
  118.5 25.2 %collective-permute-start = (bf16[448,1024]{1,0:T(8,128)(2,1)S(1)}, bf16[448,1024]{1,0:T(8,128)(2,1)S(1)}, u32[]{:S(2)}, u32[]{:S(2)}) collective-permute-start(bf16[448,1024]{1,0:T(8,128)(2,1)S(1)} %slice.13), channel_id=1, source_target_pairs={{0,16},{2,18},{4,20},{6,22},{8,24},{10,26},{12,28},{14,30},{1,17},... | collective-permute-start | bytes 2752520 | tf_op jit(solution)/shard_map/ppermute | solution.py:19
  143.7 0.9 copy-start.8
  149.8 281.8 %all-reduce.8.cloned.1.call-start = ((), (), s32[]{:S(2)}) async-start(), calls=%async_computation.2 | async-start | bytes 3670016 | tf_op jit(solution)/shard_map/psum | solution.py:99
  310.9 6.3 %copy-start.7 = (bf16[1024,1792]{1,0:T(8,128)(2,1)S(1)}, bf16[1024,1792]{1,0:T(8,128)(2,1)}, u32[]{:S(2)}) copy-start(bf16[1024,1792]{1,0:T(8,128)(2,1)} %param.19) | copy-start | bytes 11010052
  315.5 1.7 copy-start.2
  320.6 42.4 %collective-permute-start.1 = (bf16[448,1024]{1,0:T(8,128)(2,1)}, bf16[448,1024]{1,0:T(8,128)(2,1)}, u32[]{:S(2)}, u32[]{:S(2)}) collective-permute-start(bf16[448,1024]{1,0:T(8,128)(2,1)} %get-tuple-element.26), channel_id=1, source_target_pairs={{16,0},{18,2},{20,4},{22,6},{24,8},{26,10},{28,12},{30,14},{17,1},... | collective-permute-start | bytes 2752520 | tf_op jit(solution)/shard_map/ppermute | solution.py:19
  373.2 62.8 %copy-start.4 = (bf16[2048]{0:T(1024)(128)(2,1)S(1)}, bf16[2048]{0:T(1024)(128)(2,1)}, u32[]{:S(2)}) copy-start(bf16[2048]{0:T(1024)(128)(2,1)} %param.23) | copy-start | bytes 12292
  373.2 62.8 %copy-start.5 = (bf16[2048]{0:T(1024)(128)(2,1)S(1)}, bf16[2048]{0:T(1024)(128)(2,1)}, u32[]{:S(2)}) copy-start(bf16[2048]{0:T(1024)(128)(2,1)} %param.22) | copy-start | bytes 12292
Sparse Core Ops, SparseCore 0:
  17.7 98.2 all-reduce.3
  149.9 160.9 all-reduce.5
  373.3 58.1 all-reduce.7
where the time goes:
time: 472 us; the launch traced here: 470 us
  waiting for transfers between devices  332 us (70%)
  matrix products  98.1 us (21%)
  other arithmetic  16.9 us (4%)
  between operations  13.9 us (3%)
  starting transfers between devices  5.3 us (1%)
    psum x1, waiting for transfers between devices, local(): recon_total = lax.psum(partial_recon, 'feat')  161 us
    psum x1, waiting for transfers between devices, local(): preact = lax.psum(partial_pre, 'width') + biases.astype(jnp.float32)  98.3 us
    dot_general x3, matrix products, over_rows(): lax.dot_general(left, right, (((0,), (0,)), ((), ())), preferred_element_...  68.9 us
    psum x1, waiting for transfers between devices, local(): lax.psum((own_back + returned_sum).astype(jnp.bfloat16), 'width')  43.6 us
    ppermute x2, waiting for transfers between devices, shifted(): lax.ppermute(value, axis, [(source, source + steps) for source in range(l...  28.5 us
    dot_general x2, matrix products, over_cols(): lax.dot_general(left, right, (((1,), (1,)), ((), ())), preferred_element_...  12.2 us
  transfers between devices with their start and end apart: 5, of which 5 were waited for; matrix products, arithmetic and copies ran while one was open for 10% of the time, Pallas kernels for 0%

commit v1 on v0

v1 whole, which is shorter than its diff:
```python
import functools
import math
import jax
import jax.numpy as jnp
from jax import lax
from jax.experimental import pallas as pl
from jax.experimental.pallas import tpu as pltpu
from jax.sharding import PartitionSpec as P

STEPS = 100


beta_one = 0.9
beta_two = 0.999
learn_rate = 0.002
adam_eps = 1e-08
weight_decay = 0.1


def adamw_update(parameter, first, second, gradient, decay_rate):
    first_new = beta_one * first.astype(jnp.float32) + (1.0 - beta_one) * gradient
    second_new = beta_two * second.astype(jnp.float32) + (1.0 - beta_two) * gradient * gradient
    first_hat = first_new / (1.0 - beta_one**STEPS)
    second_hat = second_new / (1.0 - beta_two**STEPS)
    weight = parameter.astype(jnp.float32)
    updated = weight - learn_rate * (
        first_hat / (jnp.sqrt(second_hat) + adam_eps) + decay_rate * weight
    )
    return (
        updated.astype(jnp.bfloat16),
        first_new.astype(jnp.bfloat16),
        second_new.astype(jnp.bfloat16),
    )


def adamw_kernel(decay_rate, tile, pieces, *refs):
    left_refs, right_refs = refs[:pieces], refs[pieces : 2 * pieces]
    weight_ref, first_ref, second_ref = refs[2 * pieces : 2 * pieces + 3]
    updated_ref, moment_ref, square_ref = refs[-3:]
    first_scale, second_scale = 1.0 - beta_one**STEPS, 1.0 - beta_two**STEPS
    keep = 1.0 - learn_rate * decay_rate
    rate = learn_rate * math.sqrt(second_scale) / first_scale
    shift = adam_eps * math.sqrt(second_scale)
    for start in range(0, weight_ref.shape[1], tile):
        columns = slice(start, start + tile)
        gradient = over_rows(left_refs[0][...], right_refs[0][:, columns])
        for left_ref, right_ref in zip(left_refs[1:], right_refs[1:]):
            gradient = gradient + over_rows(left_ref[...], right_ref[:, columns])
        scaled = (1.0 - beta_one) * gradient
        first_new = beta_one * first_ref[:, columns].astype(jnp.float32) + scaled
        second_new = (
            beta_two * second_ref[:, columns].astype(jnp.float32)
            + ((1.0 - beta_two) * gradient) * gradient
        )
        root = second_new * lax.rsqrt(second_new)
        step = (rate * first_new) * pl.reciprocal(root + shift, approx=True)
        updated = keep * weight_ref[:, columns].astype(jnp.float32) - step
        updated_ref[:, columns] = updated.astype(jnp.bfloat16)
        moment_ref[:, columns] = first_new.astype(jnp.bfloat16)
        square_ref[:, columns] = second_new.astype(jnp.bfloat16)


def adamw_matmul(
    lefts, rights, weight, first, second, decay_rate, share=(0, 1), partly_done=()
):
    rows, width = weight.shape
    block = math.gcd(rows // share[1], 256)
    count = rows // share[1] // block
    base = share[0] * count
    tile = math.gcd(width, 256)
    strip = pl.BlockSpec((block, width), lambda place: (base + place, 0))
    left_specs = [
        pl.BlockSpec((left.shape[0], block), lambda place: (0, base + place)) for left in lefts
    ]
    right_specs = [pl.BlockSpec(right.shape, lambda place: (0, 0)) for right in rights]
    tokens = sum(left.shape[0] for left in lefts)
    return pl.pallas_call(
        functools.partial(adamw_kernel, decay_rate, tile, len(lefts)),
        grid=(count,),
        in_specs=left_specs
        + right_specs
        + [strip] * 3
        + [pl.BlockSpec(memory_space=pl.ANY)] * len(partly_done),
        out_specs=[strip] * 3,
        out_shape=[jax.ShapeDtypeStruct((rows, width), jnp.bfloat16)] * 3,
        input_output_aliases={2 * len(lefts) + 3 + at: at for at in range(len(partly_done))},
        compiler_params=pltpu.CompilerParams(vmem_limit_bytes=40 * 2**20),
        cost_estimate=pl.CostEstimate(
            flops=2 * tokens * block * count * width,
            bytes_accessed=12 * block * count * width,
            transcendentals=2 * block * count * width,
        ),
    )(*lefts, *rights, weight, first, second, *partly_done)


def matmul(left, right):
    return jnp.dot(left, right, preferred_element_type=jnp.float32)


def over_rows(left, right):
    return lax.dot_general(
        left, right, (((0,), (0,)), ((), ())), preferred_element_type=jnp.float32
    )


def over_cols(left, right):
    return lax.dot_general(
        left, right, (((1,), (1,)), ((), ())), preferred_element_type=jnp.float32
    )


def across(value):
    return lax.ppermute(value, "width", [(0, 1), (1, 0)])


def flipped(value, bit, members):
    step = 1 << bit
    return lax.ppermute(value, "feat", [(index, index ^ step) for index in range(members)])


def halves(value, axis):
    size = value.shape[axis] // 2
    return lax.slice_in_dim(value, 0, size, axis=axis), lax.slice_in_dim(
        value, size, 2 * size, axis=axis
    )


def is_upper(bit):
    return ((lax.axis_index("feat") >> bit) & 1) == 1


def split_for(total, bit, axis):
    low, high = halves(total, axis)
    upper = is_upper(bit)
    return jnp.where(upper, high, low), jnp.where(upper, low, high).astype(jnp.bfloat16)


def joined(own, other, bit, axis):
    upper = is_upper(bit)
    return jnp.concatenate(
        [jnp.where(upper, other, own), jnp.where(upper, own, other)], axis=axis
    )


def plan_of(order):
    last = len(order) - 1
    return [
        (bit, None if place == last else 1 if place == 2 else 0)
        for place, bit in enumerate(order)
    ]


def sent_block(total, step, members):
    bit, axis = step
    if axis is None:
        return total, flipped(total.astype(jnp.bfloat16), bit, members)
    keeping, leaving = split_for(total, bit, axis)
    return keeping, flipped(leaving, bit, members)


def ordered(*groups):
    return lax.optimization_barrier(groups)


class Order:
    def __init__(self, threads):
        self.threads = threads
        self.waiting = [next(thread)[1] for thread in threads]
        self.last = ()

    def advance(self, which):
        inputs, _ = ordered(self.waiting[which], self.last)
        self.last, self.waiting[which] = self.threads[which].send(inputs)

    def after(self, values):
        return ordered(values, self.last)[0]


def local(
    residual,
    targets,
    encoder,
    biases,
    same_decoder,
    next_decoder,
    encoder_first,
    encoder_second,
    biases_first,
    biases_second,
    same_first,
    same_second,
    next_first,
    next_second,
):
    feat_count = lax.axis_size("feat")
    feat_index = lax.axis_index("feat")
    width_index = lax.axis_index("width")
    half_count = feat_count // 2
    source_layer = feat_index // half_count
    leading = source_layer == 0
    tokens, width = residual.shape[1:]
    chunks = 2
    part = tokens // (2 * chunks)
    half = encoder.shape[1] // 2
    bias = biases.astype(jnp.float32)
    downward = [(index, index + half_count) for index in range(half_count)]
    upward = [(index + half_count, index) for index in range(half_count)]
    trailing_pairs = [
        (2 * index + side, 2 * index + 1 - side)
        for index in range(half_count, feat_count)
        for side in range(2)
    ]

    def rows_of(chunk):
        blocks = [
            lax.dynamic_slice(
                residual,
                (source_layer, side * (tokens // 2) + chunk * part, 0),
                (1, part, width),
            )
            for side in (width_index, 1 - width_index)
        ]
        return jnp.concatenate(blocks, axis=1)[0]

    def wanted_block(layer, chunk, plan):
        starts, sizes = [0, 0], [2 * part, width]
        for bit, axis in plan:
            if axis is not None:
                sizes[axis] //= 2
                starts[axis] = starts[axis] + is_upper(bit).astype(jnp.int32) * sizes[axis]
        side = jnp.where(starts[0] >= part, 1 - width_index, width_index)
        row = side * (tokens // 2) + chunk * part + lax.rem(starts[0], part)
        block = lax.dynamic_slice(targets, (layer, row, starts[1]), (1, *sizes))
        return block[0].astype(jnp.float32)

    inputs = [rows_of(chunk) for chunk in range(chunks)]
    bits = feat_count.bit_length() - 1
    second_plan = plan_of(list(range(bits)))
    first_plan = plan_of([0, 2, 1] + list(range(3, bits - 1)))
    def add(total, arrived):
        return total + arrived.astype(jnp.float32)

    def stages_of(layer, plan):
        moves = [("sum", *step) for step in plan[1:]]
        backward = [("join", *step) for step in reversed(plan[1:]) if step[1] is not None]
        return [(layer, plan, move) for move in moves + backward]

    stages = [stages_of(0, first_plan), stages_of(1, second_plan)]
    members = [half_count, feat_count]

    def settle(layer, place, chunk, value, other):
        if place > len(stages[layer]):
            return value
        before = stages[layer][place - 1][2] if place > 0 else ("sum",)
        last_sum = len([0 for stage in stages[layer] if stage[2][0] == "sum"])
        if before[0] == "sum":
            value = add(value, other)
            if place == last_sum:
                plan = (first_plan, second_plan)[layer]
                value = (value - wanted_block(layer, chunk, plan)).astype(jnp.bfloat16)
            return value
        return joined(value, other, *before[1:])

    def move(layer, place, value):
        if place >= len(stages[layer]):
            return value, value
        kind, bit, axis = stages[layer][place][2]
        if kind == "sum":
            return sent_block(value, (bit, axis), members[layer])
        return value, flipped(value, bit, members[layer])

    def chunk_steps(chunk):
        (given,) = yield (), (inputs[chunk],)
        partial_pre = matmul(given, encoder)
        leaving = partial_pre[part:].astype(jnp.float16)
        keeping, arriving = yield (leaving,), (partial_pre[:part], across(leaving))
        pre = add(keeping, arriving) + bias
        shared = jnp.maximum(pre, 0.0).astype(jnp.bfloat16)
        sent = lax.ppermute(shared[:, half:], "feat", downward)
        shared, other, sent = yield (shared,), (shared, across(shared), sent)
        sent_other = lax.ppermute(sent, ("feat", "width"), trailing_pairs)
        active = jnp.concatenate([shared, other], axis=0)
        own_term = matmul(active, same_decoder)
        sent, sent_other, own_term = yield (own_term,), (sent, sent_other, own_term)
        sent_full = jnp.concatenate([sent, sent_other], axis=0)
        cross_input = jnp.where(leading, active[:, :half], sent_full)
        cross_term = matmul(cross_input, next_decoder)
        second_part = jnp.where(leading, cross_term, own_term + cross_term)
        values, leaves = zip(*[split_for(own_term, 0, 0), split_for(second_part, 0, 0)])
        leaving = jnp.concatenate(leaves, axis=0)
        values, arriving = yield (leaving,), (values, flipped(leaving, 0, feat_count))
        others = halves(arriving, 0)
        for place in range(len(stages[1])):
            values = [settle(layer, place, chunk, values[layer], others[layer]) for layer in (0, 1)]
            values, others = zip(*[move(layer, place, values[layer]) for layer in (0, 1)])
            values, others = yield values, (values, others)
        place = len(stages[1])
        values = [settle(layer, place, chunk, values[layer], others[layer]) for layer in (0, 1)]
        both = jnp.concatenate(values, axis=0)
        values, arriving = yield (both,), (values, flipped(both, 0, feat_count))
        others = halves(arriving, 0)
        delta_first, delta_next = [joined(values[layer], others[layer], 0, 0) for layer in (0, 1)]
        delta_own = jnp.where(leading, delta_first, delta_next)
        cross_back = over_cols(delta_next, next_decoder)
        cross_leaving = cross_back[part:].astype(jnp.bfloat16)
        cross_arriving = lax.ppermute(cross_leaving, ("feat", "width"), trailing_pairs)
        back = over_cols(delta_own, same_decoder)
        back_a = back[:, :half] + jnp.where(leading, cross_back, 0.0)
        back = jnp.concatenate([back_a, back[:, half:]], axis=1)
        leaving = back[part:].astype(jnp.bfloat16)
        arriving = across(leaving)
        grads[chunk] = (active, delta_own, cross_input, delta_next)
        cross_keeping, cross_arriving = yield (leaving,), (cross_back[:part], cross_arriving)
        cross_sum = add(cross_keeping, cross_arriving).astype(jnp.bfloat16)
        returned = lax.ppermute(cross_sum, "feat", upward)
        keeping, arriving, returned = yield (cross_sum,), (back[:part], arriving, returned)
        total = add(keeping, arriving)
        total = jnp.concatenate([total[:, :half], add(total[:, half:], returned)], axis=1)
        shared = jnp.where(pre > 0.0, total, 0.0).astype(jnp.bfloat16)
        sums[chunk] = jnp.sum(shared.astype(jnp.float32), axis=0)
        shared, other = yield (shared,), (shared, across(shared))
        preact_grad[chunk] = jnp.concatenate([shared, other], axis=0)
        yield (preact_grad[chunk],), ()

    grads, sums, preact_grad = {}, {}, {}
    order = Order([chunk_steps(0), chunk_steps(1)])
    steps = len(stages[1]) + 9
    turns = [0, 0, 1, 0, 0, 1, 0, 0, 1, 0, 0, 1]
    turns += [0, 1] * (steps - turns.count(0))
    for which in turns:
        order.advance(which)
    for _ in range(steps - 3 - turns.count(1)):
        order.advance(1)

    active, delta_own, cross_input, delta_next = zip(grads[0], grads[1])
    next_done = adamw_matmul(
        cross_input, delta_next, next_decoder, next_first, next_second, weight_decay
    )
    order.last = next_done
    order.advance(1)
    same_done = adamw_matmul(
        active, order.after(delta_own), same_decoder, same_first, same_second, weight_decay, (0, 2)
    )
    order.last = same_done
    order.advance(1)
    same_done = adamw_matmul(
        active,
        order.after(delta_own),
        same_decoder,
        same_first,
        same_second,
        weight_decay,
        (1, 2),
        same_done,
    )
    order.last = same_done
    order.advance(1)
    grad_sum = sums[0] + sums[1]
    grad_biases = grad_sum + across(grad_sum)
    updated_same, same_moment, same_square = same_done
    updated_next, next_moment, next_square = next_done
    updated_encoder, encoder_moment, encoder_square = adamw_matmul(
        inputs,
        (preact_grad[0], preact_grad[1]),
        encoder,
        encoder_first,
        encoder_second,
        weight_decay,
    )
    updated_biases, biases_moment, biases_square = adamw_update(
        biases, biases_first, biases_second, grad_biases, 0.0
    )
    return (
        updated_encoder,
        updated_biases,
        updated_same,
        updated_next,
        encoder_moment,
        encoder_square,
        biases_moment,
        biases_square,
        same_moment,
        same_square,
        next_moment,
        next_square,
    )


def solution(mesh):
    in_specs = (
        P(None, None, "width"),
        P(None, None, "width"),
        P("width", "feat"),
        P("feat"),
        P("feat", "width"),
        P("feat", "width"),
        P("width", "feat"),
        P("width", "feat"),
        P("feat"),
        P("feat"),
        P("feat", "width"),
        P("feat", "width"),
        P("feat", "width"),
        P("feat", "width"),
    )
    out_specs = (
        P("width", "feat"),
        P("feat"),
        P("feat", "width"),
        P("feat", "width"),
        P("width", "feat"),
        P("width", "feat"),
        P("feat"),
        P("feat"),
        P("feat", "width"),
        P("feat", "width"),
        P("feat", "width"),
        P("feat", "width"),
    )
    return jax.shard_map(local, mesh=mesh, in_specs=in_specs, out_specs=out_specs, check_vma=False)
```

time: 472 us -> 224 us (0.47)
  waiting for transfers between devices: 332 us -> 63.4 us
  matrix products: 98.1 us -> 24.3 us
  starting transfers between devices: 5.3 us -> 60 us
  Pallas kernels: 0 us -> 47.7 us
  between operations: 13.9 us -> 1.89 us
    psum x3 -> x0, waiting for transfers between devices: 303 us -> none  [the longest x1 161 us: local(): recon_total = lax.psum(partial_recon, 'feat')]
    dot_general x6, matrix products: 85.9 us -> 17.4 us  [matmul(): return jnp.dot(left, right, preferred_element_type=jnp.float32)]
    ppermute x2 -> x37, starting transfers between devices: 5.18 us -> 60 us  [the longest x20 27.2 us: flipped(): lax.ppermute(value, 'feat', [(index, index ^ step) for index in range(mem...]
    pallas_call x0 -> x4, Pallas kernels: none -> 47.7 us  [adamw_matmul(): pl.pallas_call(functools.partial(adamw_kernel, decay_rate, tile, len(left...]
    ppermute x2 -> x37, waiting for transfers between devices: 28.5 us -> 63.4 us  [the longest x20 30.4 us: flipped(): lax.ppermute(value, 'feat', [(index, index ^ step) for index in range(mem...]
    dot_general x2 -> x4, matrix products: 12.2 us -> 6.99 us  [over_cols(): lax.dot_general(left, right, (((1,), (1,)), ((), ())), preferred_element_...]
  transfers between devices with their start and end apart: 5 -> 37, of which waited for: 5 -> 15; matrix products, arithmetic and copies ran while one was open for 10% -> 14% of each run, Pallas kernels for 0% -> 13%
where the time goes in v1:
time: 224 us; the launch traced here: 221 us
  waiting for transfers between devices  63.4 us (28%)
  starting transfers between devices  60 us (27%)
  Pallas kernels  47.7 us (21%)
  matrix products  24.3 us (11%)
  other arithmetic  16.9 us (8%)
  local copies, waits for them, and re-layouts  7.17 us (3%)
    pallas_call x4, Pallas kernels, adamw_matmul(): pl.pallas_call(functools.partial(adamw_kernel, decay_rate, tile, len(left...  47.7 us
    ppermute x20, waiting for transfers between devices, flipped(): lax.ppermute(value, 'feat', [(index, index ^ step) for index in range(mem...  30.4 us
    ppermute x20, starting transfers between devices, flipped(): lax.ppermute(value, 'feat', [(index, index ^ step) for index in range(mem...  27.2 us
    ppermute x9, waiting for transfers between devices, across(): return lax.ppermute(value, 'width', [(0, 1), (1, 0)])  21.1 us
    dot_general x6, matrix products, matmul(): return jnp.dot(left, right, preferred_element_type=jnp.float32)  17.4 us
    ppermute x9, starting transfers between devices, across(): return lax.ppermute(value, 'width', [(0, 1), (1, 0)])  11.1 us
    ppermute x2, waiting for transfers between devices, chunk_steps(): sent_other = lax.ppermute(sent, ('feat', 'width'), trailing_pairs)  7.77 us
    dot_general x4, matrix products, over_cols(): lax.dot_general(left, right, (((1,), (1,)), ((), ())), preferred_element_...  6.99 us
  transfers between devices with their start and end apart: 37, of which 15 were waited for; matrix products, arithmetic and copies ran while one was open for 14% of the time, Pallas kernels for 13%

profile of v1, /device:TPU:20, one launch (start us, length us, event | category | flops | bytes accessed | tf_op | source)
XLA Modules:
  0.0 221.4 jit_solution(10876783690641275970)
XLA Ops:
  0.7 1.5 constant_dynamic-slice_fusion.1
  2.3 4.9 %fusion.26 = f32[224,2048]{1,0:T(8,128)S(1)} fusion(bf16[224,1792]{1,0:T(8,128)(2,1)S(1)} %get-tuple-element.265.refs_0_, bf16[1792,2048]{1,0:T(8,128)(2,1)} %refs_4_.7), kind=kOutput, calls=%fused_computation.138 | convolution fusion | flops 1644167168 | bytes 9977856 | tf_op jit(solution)/shard_map/dot_general | solution.py:97
  7.4 1.6 collective-permute-start
  8.9 10.8 %collective-permute-done = f16[112,2048]{1,0:T(8,128)(2,1)S(1)} collective-permute-done((f16[112,2048]{1,0:T(8,128)(2,1)S(1)}, f16[112,2048]{1,0:T(8,128)(2,1)S(1)}, u32[]{:S(2)}, u32[]{:S(2)}) %collective-permute-start) | collective-permute-done | bytes 458784 | tf_op jit(solution)/shard_map/ppermute | solution.py:113
  19.9 1.6 collective-permute-start.1
  21.4 1.5 collective-permute-start.2
  23.0 5.5 %fusion.27 = f32[224,2048]{1,0:T(8,128)S(1)} fusion(bf16[224,1792]{1,0:T(8,128)(2,1)S(1)} %get-tuple-element.109.refs_1_, bf16[1792,2048]{1,0:T(8,128)(2,1)} %refs_4_.7), kind=kOutput, calls=%fused_computation.139 | convolution fusion | flops 1644167168 | bytes 9977856 | tf_op jit(solution)/shard_map/dot_general | solution.py:97
  29.3 1.5 collective-permute-done.2
  30.8 1.8 collective-permute-done.1
  32.6 4.2 %collective-permute-start.3 = (bf16[112,1024]{1,0:T(8,128)(2,1)S(1)}, bf16[112,1024]{1,0:T(8,128)(2,1)S(1)}, u32[]{:S(2)}, u32[]{:S(2)}) collective-permute-start(bf16[112,1024]{1,0:T(8,128)(2,1)S(1)} %collective-permute-done.2), channel_id=1, source_target_pairs={{16,17},{17,16},{18,19},{19,18},{20,21},{21,20},{22,23},{23,22},{2... | collective-permute-start | bytes 688136 | tf_op jit(solution)/shard_map/ppermute | solution.py:281
  36.9 1.9 fusion.28
  38.8 7.3 %collective-permute-done.3 = bf16[112,1024]{1,0:T(8,128)(2,1)S(1)} collective-permute-done((bf16[112,1024]{1,0:T(8,128)(2,1)S(1)}, bf16[112,1024]{1,0:T(8,128)(2,1)S(1)}, u32[]{:S(2)}, u32[]{:S(2)}) %collective-permute-start.3) | collective-permute-done | bytes 229408 | tf_op jit(solution)/shard_map/ppermute | solution.py:281
  46.3 1.0 add_select_fusion.1
  47.7 1.6 collective-permute-start.10
  49.3 1.3 collective-permute-start.11
  50.8 0.8 collective-permute-done.4
  53.2 6.5 %collective-permute-done.7 = bf16[56,1792]{1,0:T(8,128)(2,1)S(1)} collective-permute-done((bf16[56,1792]{1,0:T(8,128)(2,1)S(1)}, bf16[56,1792]{1,0:T(8,128)(2,1)S(1)}, u32[]{:S(2)}, u32[]{:S(2)}) %collective-permute-start.7) | collective-permute-done | bytes 200736 | tf_op jit(solution)/shard_map/ppermute | solution.py:118
  60.5 5.9 %collective-permute-start.9 = (bf16[56,896]{1,0:T(8,128)(2,1)S(1)}, bf16[56,896]{1,0:T(8,128)(2,1)S(1)}, u32[]{:S(2)}, u32[]{:S(2)}) collective-permute-start(bf16[56,896]{1,0:T(8,128)(2,1)S(1)} %select_convert_fusion.9), channel_id=1, source_target_pairs={{0,8},{2,10},{4,12},{6,14},{8,0},{10,2},{12,4},{14,6},{16,24},{18,... | collective-permute-start | bytes 301064 | tf_op jit(solution)/shard_map/ppermute | solution.py:118
  66.5 3.0 %fusion.29 = f32[224,1792]{1,0:T(8,128)} fusion(bf16[224,2048]{1,0:T(8,128)(2,1)S(1)} %constant_dynamic-update-slice_fusion.2.refs_1_, bf16[2048,1792]{1,0:T(8,128)(2,1)S(1)} %bitcast.35), kind=kOutput, calls=%fused_computation.141 | convolution fusion | flops 1644167168 | bytes 9863168 | tf_op jit(solution)/shard_map/dot_general | solution.py:97
  69.6 1.7 fusion.7
  71.3 1.4 collective-permute-start.12
  73.4 6.0 %collective-permute-start.13 = (bf16[56,896]{1,0:T(8,128)(2,1)}, bf16[56,896]{1,0:T(8,128)(2,1)}, u32[]{:S(2)}, u32[]{:S(2)}) collective-permute-start(bf16[56,896]{1,0:T(8,128)(2,1)} %get-tuple-element.210), channel_id=1, source_target_pairs={{0,16},{2,18},{4,20},{6,22},{8,24},{10,26},{12,28},{14,30},{16,0},... | collective-permute-start | bytes 301064 | tf_op jit(solution)/shard_map/ppermute | solution.py:118
  79.4 2.7 %collective-permute-start.15 = (bf16[112,1024]{1,0:T(8,128)(2,1)}, bf16[112,1024]{1,0:T(8,128)(2,1)S(1)}, u32[]{:S(2)}, u32[]{:S(2)}) collective-permute-start(bf16[112,1024]{1,0:T(8,128)(2,1)} %copy-done.19), channel_id=1, source_target_pairs={{16,17},{17,16},{18,19},{19,18},{20,21},{21,20},{22,23},{23,22},{2... | collective-permute-start | bytes 688136 | tf_op jit(solution)/shard_map/ppermute | solution.py:281
  82.1 2.7 %collective-permute-done.13 = bf16[56,896]{1,0:T(8,128)(2,1)} collective-permute-done((bf16[56,896]{1,0:T(8,128)(2,1)}, bf16[56,896]{1,0:T(8,128)(2,1)}, u32[]{:S(2)}, u32[]{:S(2)}) %collective-permute-start.13) | collective-permute-done | bytes 100384 | tf_op jit(solution)/shard_map/ppermute | solution.py:118
  84.8 1.2 fusion.9
  86.0 1.1 broadcast_select_fusion.15
  88.2 1.5 copy-done.1
  89.8 1.0 add_select_fusion
  91.7 1.6 collective-permute-done.17
  93.6 5.0 %collective-permute-done.16 = bf16[56,1792]{1,0:T(8,128)(2,1)S(1)} collective-permute-done((bf16[56,1792]{1,0:T(8,128)(2,1)S(1)}, bf16[56,1792]{1,0:T(8,128)(2,1)S(1)}, u32[]{:S(2)}, u32[]{:S(2)}) %collective-permute-start.16) | collective-permute-done | bytes 200736 | tf_op jit(solution)/shard_map/ppermute | solution.py:118
  100.1 5.9 %collective-permute-done.20 = bf16[56,1792]{1,0:T(8,128)(2,1)S(1)} collective-permute-done((bf16[56,1792]{1,0:T(8,128)(2,1)S(1)}, bf16[56,1792]{1,0:T(8,128)(2,1)S(1)}, u32[]{:S(2)}, u32[]{:S(2)}) %collective-permute-start.20) | collective-permute-done | bytes 200736 | tf_op jit(solution)/shard_map/ppermute | solution.py:118
  106.7 1.6 collective-permute-start.24
  108.5 1.2 fusion.14
  109.8 2.7 %collective-permute-start.22 = (bf16[112,1024]{1,0:T(8,128)(2,1)S(1)}, bf16[112,1024]{1,0:T(8,128)(2,1)S(1)}, u32[]{:S(2)}, u32[]{:S(2)}) collective-permute-start(bf16[112,1024]{1,0:T(8,128)(2,1)S(1)} %slice.329), channel_id=1, source_target_pairs={{16,17},{17,16},{18,19},{19,18},{20,21},{21,20},{22,23},{23,22},{2... | collective-permute-start | bytes 688136 | tf_op jit(solution)/shard_map/ppermute | solution.py:306
  112.8 2.3 %fusion.30 = f32[224,2048]{1,0:T(8,128)S(1)} fusion(bf16[224,1792]{1,0:T(8,128)(2,1)S(1)} %get-tuple-element.192.refs_2_, bf16[2048,1792]{1,0:T(8,128)(2,1)S(1)} %bitcast.37), kind=kOutput, calls=%fused_computation.142 | convolution fusion | flops 1644167168 | bytes 9977856 | tf_op jit(solution)/shard_map/dot_general | solution.py:107
  115.4 1.6 collective-permute-start.21
  116.9 1.0 fusion.6
  118.0 0.8 collective-permute-start.26
  118.8 5.5 %collective-permute-start.27 = (bf16[56,896]{1,0:T(8,128)(2,1)S(1)}, bf16[56,896]{1,0:T(8,128)(2,1)S(1)}, u32[]{:S(2)}, u32[]{:S(2)}) collective-permute-start(bf16[56,896]{1,0:T(8,128)(2,1)S(1)} %get-tuple-element.206), channel_id=1, source_target_pairs={{0,16},{2,18},{4,20},{6,22},{8,24},{10,26},{12,28},{14,30},{16,0},... | collective-permute-start | bytes 301064 | tf_op jit(solution)/shard_map/ppermute | solution.py:118
  124.5 1.9 collective-permute-start.25
  126.4 5.8 %collective-permute-done.27 = bf16[56,896]{1,0:T(8,128)(2,1)S(1)} collective-permute-done((bf16[56,896]{1,0:T(8,128)(2,1)S(1)}, bf16[56,896]{1,0:T(8,128)(2,1)S(1)}, u32[]{:S(2)}, u32[]{:S(2)}) %collective-permute-start.27) | collective-permute-done | bytes 100384 | tf_op jit(solution)/shard_map/ppermute | solution.py:118
  132.3 1.0 fusion.8
  133.4 2.5 %collective-permute-done.25 = bf16[112,1024]{1,0:T(8,128)(2,1)S(1)} collective-permute-done((bf16[112,1024]{1,0:T(8,128)(2,1)S(1)}, bf16[112,1024]{1,0:T(8,128)(2,1)S(1)}, u32[]{:S(2)}, u32[]{:S(2)}) %collective-permute-start.25) | collective-permute-done | bytes 229408 | tf_op jit(solution)/shard_map/ppermute | solution.py:315
  136.4 1.6 collective-permute-start.28
  138.1 1.3 collective-permute-start.30
  139.3 8.5 %collective-permute-done.28 = bf16[112,2048]{1,0:T(8,128)(2,1)S(1)} collective-permute-done((bf16[112,2048]{1,0:T(8,128)(2,1)S(1)}, bf16[112,2048]{1,0:T(8,128)(2,1)S(1)}, u32[]{:S(2)}, u32[]{:S(2)}) %collective-permute-start.28) | collective-permute-done | bytes 458784 | tf_op jit(solution)/shard_map/ppermute | solution.py:113
  148.2 2.3 %collective-permute-done.31 = bf16[224,1792]{1,0:T(8,128)(2,1)S(1)} collective-permute-done((bf16[224,1792]{1,0:T(8,128)(2,1)S(1)}, bf16[224,1792]{1,0:T(8,128)(2,1)S(1)}, u32[]{:S(2)}, u32[]{:S(2)}) %collective-permute-start.31) | collective-permute-done | bytes 802848 | tf_op jit(solution)/shard_map/ppermute | solution.py:118
  150.6 1.2 fusion.13
  151.8 0.7 slice.328
  152.6 3.4 %collective-permute-start.33 = (bf16[112,1024]{1,0:T(8,128)(2,1)}, bf16[112,1024]{1,0:T(8,128)(2,1)}, u32[]{:S(2)}, u32[]{:S(2)}) collective-permute-start(bf16[112,1024]{1,0:T(8,128)(2,1)} %slice.328), channel_id=1, source_target_pairs={{16,17},{17,16},{18,19},{19,18},{20,21},{21,20},{22,23},{23,22},{2... | collective-permute-start | bytes 688136 | tf_op jit(solution)/shard_map/ppermute | solution.py:306
  156.2 2.3 %fusion.31 = f32[224,2048]{1,0:T(8,128)S(1)} fusion(bf16[224,1792]{1,0:T(8,128)(2,1)S(1)} %get-tuple-element.193.refs_3_, bf16[2048,1792]{1,0:T(8,128)(2,1)S(1)} %bitcast.37), kind=kOutput, calls=%fused_computation.143 | convolution fusion | flops 1644167168 | bytes 9977856 | tf_op jit(solution)/shard_map/dot_general | solution.py:107
  158.7 0.9 copy-done.15
  159.7 0.8 fusion.2
  160.5 0.8 slice.250
  162.3 7.9 %shard_map.229 = (bf16[1024,1792]{1,0:T(8,128)(2,1)}, bf16[1024,1792]{1,0:T(8,128)(2,1)}, bf16[1024,1792]{1,0:T(8,128)(2,1)}) custom-call(bf16[224,1024]{1,0:T(8,128)(2,1)S(1)} %slice_select_fusion.5.refs_0_, bf16[224,1024]{1,0:T(8,128)(2,1)S(1)} %slice_select_fusion.4.refs_1_, bf16[224,1792]{1,0:T(8,128)(2,1)S(1)} %get-tuple-element.240.refs_2_, ...), custom_call_target="tpu_custom_call" | custom-call | flops 1644167168 | bytes 22020096 | tf_op jit(solution)/shard_map/pallas_call | solution.py:77
  170.2 1.3 add_convert_fusion
  171.5 4.0 %collective-permute-start.34 = (bf16[112,1024]{1,0:T(8,128)(2,1)S(1)}, bf16[112,1024]{1,0:T(8,128)(2,1)S(1)}, u32[]{:S(2)}, u32[]{:S(2)}) collective-permute-start(bf16[112,1024]{1,0:T(8,128)(2,1)S(1)} %add_convert_fusion), channel_id=1, source_target_pairs={{16,0},{18,2},{20,4},{22,6},{24,8},{26,10},{28,12},{30,14},{17,1},... | collective-permute-start | bytes 688136 | tf_op jit(solution)/shard_map/ppermute | solution.py:315
  175.4 1.1 fusion
  176.6 10.3 %shard_map.230 = (bf16[2048,1792]{1,0:T(8,128)(2,1)}, bf16[2048,1792]{1,0:T(8,128)(2,1)}, bf16[2048,1792]{1,0:T(8,128)(2,1)}) custom-call(bf16[224,2048]{1,0:T(8,128)(2,1)S(1)} %copy-done.3, bf16[224,2048]{1,0:T(8,128)(2,1)S(1)} %copy-done.5, bf16[224,1792]{1,0:T(8,128)(2,1)S(1)} %get-tuple-element.192.refs_2_, ...), custom_call_target="tpu_custom_call" | custom-call | flops 1644167168 | bytes 22020096 | tf_op jit(solution)/shard_map/pallas_call | solution.py:77
  186.9 1.2 convert_add_fusion
  188.6 1.1 collective-permute-start.35
  189.6 1.1 collective-permute-start.36
  190.7 10.8 %shard_map.231 = (bf16[2048,1792]{1,0:T(8,128)(2,1)}, bf16[2048,1792]{1,0:T(8,128)(2,1)}, bf16[2048,1792]{1,0:T(8,128)(2,1)}) custom-call(bf16[224,2048]{1,0:T(8,128)(2,1)S(1)} %copy-done.3, bf16[224,2048]{1,0:T(8,128)(2,1)S(1)} %copy-done.5, ...), custom_call_target="tpu_custom_call", output_to_operand_aliasing={{0}: (7, {}), {1}: (8, {}), {2}: (9, {})} | custom-call | flops 1644167168 | bytes 22020096 | tf_op jit(solution)/shard_map/pallas_call | solution.py:77
  202.8 18.6 %shard_map.232 = (bf16[1792,2048]{1,0:T(8,128)(2,1)}, bf16[1792,2048]{1,0:T(8,128)(2,1)}, bf16[1792,2048]{1,0:T(8,128)(2,1)}) custom-call(bf16[224,1792]{1,0:T(8,128)(2,1)S(1)} %get-tuple-element.265.refs_0_, bf16[224,1792]{1,0:T(8,128)(2,1)S(1)} %get-tuple-element.109.refs_1_, bf16[224,2048]{1,0:T(8,128)(2,1)S(1)} %copy-done.9, ...), custom_call_target="tpu_custom_call" | custom-call | flops 3288334336 | bytes 44040192 | tf_op jit(solution)/shard_map/pallas_call | solution.py:77
  (178 shorter events, 14.7 us)
Async XLA Ops:
  7.2 1.7 copy-start.21
  7.3 21.1 %copy-start.13 = (f32[112,2048]{1,0:T(8,128)}, f32[112,2048]{1,0:T(8,128)S(1)}, u32[]{:S(2)}) copy-start(f32[112,2048]{1,0:T(8,128)S(1)} %get-tuple-element.107) | copy-start | bytes 2752516
  7.4 12.3 %collective-permute-start = (f16[112,2048]{1,0:T(8,128)(2,1)S(1)}, f16[112,2048]{1,0:T(8,128)(2,1)S(1)}, u32[]{:S(2)}, u32[]{:S(2)}) collective-permute-start(f16[112,2048]{1,0:T(8,128)(2,1)S(1)} %get-tuple-element.224), channel_id=1, source_target_pairs={{0,1},{1,0},{2,3},{3,2},{4,5},{5,4},{6,7},{7,6},{8,9},{9,8},{10,11... | collective-permute-start | bytes 1376264 | tf_op jit(solution)/shard_map/ppermute | solution.py:113
  19.9 12.7 %collective-permute-start.1 = (bf16[112,2048]{1,0:T(8,128)(2,1)S(1)}, bf16[112,2048]{1,0:T(8,128)(2,1)S(1)}, u32[]{:S(2)}, u32[]{:S(2)}) collective-permute-start(bf16[112,2048]{1,0:T(8,128)(2,1)S(1)} %maximum_convert_fusion.1), channel_id=1, source_target_pairs={{0,1},{1,0},{2,3},{3,2},{4,5},{5,4},{6,7},{7,6},{8,9},{9,8},{10,11... | collective-permute-start | bytes 1376264 | tf_op jit(solution)/shard_map/ppermute | solution.py:113
  21.4 15.4 %slice-start = ((s8[7340032]{0:T(1024)(128)(4,1)}), s8[4194304]{0:T(1024)(128)(4,1)S(1)}, s32[]{:S(2)}) async-start(s8[7340032]{0:T(1024)(128)(4,1)} %bitcast.34), calls=%async_computation | async-start | bytes 8388608
  21.4 15.4 %slice-start.1 = ((s8[7340032]{0:T(1024)(128)(4,1)}), s8[3145728]{0:T(1024)(128)(4,1)S(1)}, s32[]{:S(2)}) async-start(s8[7340032]{0:T(1024)(128)(4,1)} %bitcast.34), calls=%async_computation.1 | async-start | bytes 6291456
  21.4 9.3 %collective-permute-start.2 = (bf16[112,1024]{1,0:T(8,128)(2,1)S(1)}, bf16[112,1024]{1,0:T(8,128)(2,1)S(1)}, u32[]{:S(2)}, u32[]{:S(2)}) collective-permute-start(bf16[112,1024]{1,0:T(8,128)(2,1)S(1)} %slice.216), channel_id=1, source_target_pairs={{0,16},{2,18},{4,20},{6,22},{8,24},{10,26},{12,28},{14,30},{1,17},... | collective-permute-start | bytes 688136 | tf_op jit(solution)/shard_map/ppermute | solution.py:279
  28.6 18.9 %copy-start.11 = (f32[112,2048]{1,0:T(8,128)}, f32[112,2048]{1,0:T(8,128)S(1)}, u32[]{:S(2)}) copy-start(f32[112,2048]{1,0:T(8,128)S(1)} %get-tuple-element.116) | copy-start | bytes 2752516
  28.7 18.9 %collective-permute-start.5 = (f16[112,2048]{1,0:T(8,128)(2,1)S(1)}, f16[112,2048]{1,0:T(8,128)(2,1)S(1)}, u32[]{:S(2)}, u32[]{:S(2)}) collective-permute-start(f16[112,2048]{1,0:T(8,128)(2,1)S(1)} %get-tuple-element.223), channel_id=1, source_target_pairs={{0,1},{1,0},{2,3},{3,2},{4,5},{5,4},{6,7},{7,6},{8,9},{9,8},{10,11... | collective-permute-start | bytes 1376264 | tf_op jit(solution)/shard_map/ppermute | solution.py:113
  32.6 13.5 %collective-permute-start.3 = (bf16[112,1024]{1,0:T(8,128)(2,1)S(1)}, bf16[112,1024]{1,0:T(8,128)(2,1)S(1)}, u32[]{:S(2)}, u32[]{:S(2)}) collective-permute-start(bf16[112,1024]{1,0:T(8,128)(2,1)S(1)} %collective-permute-done.2), channel_id=1, source_target_pairs={{16,17},{17,16},{18,19},{19,18},{20,21},{21,20},{22,23},{23,22},{2... | collective-permute-start | bytes 688136 | tf_op jit(solution)/shard_map/ppermute | solution.py:281
  36.9 9.3 %copy-start.2 = (bf16[224,2048]{1,0:T(8,128)(2,1)}, bf16[224,2048]{1,0:T(8,128)(2,1)S(1)}, u32[]{:S(2)}) copy-start(bf16[224,2048]{1,0:T(8,128)(2,1)S(1)} %constant_dynamic-update-slice_fusion.refs_0_) | copy-start | bytes 2752516
  36.9 9.4 %copy-start = (bf16[1024,1792]{1,0:T(8,128)(2,1)S(1)}, bf16[1024,1792]{1,0:T(8,128)(2,1)}, u32[]{:S(2)}) copy-start(bf16[1024,1792]{1,0:T(8,128)(2,1)} %refs_4_.4) | copy-start | bytes 11010052
  47.5 3.1 %copy-start.17 = (f16[112,2048]{1,0:T(8,128)(2,1)}, f16[112,2048]{1,0:T(8,128)(2,1)S(1)}, u32[]{:S(2)}) copy-start(f16[112,2048]{1,0:T(8,128)(2,1)S(1)} %collective-permute-done.5) | copy-start | bytes 1376260
  47.7 12.8 %collective-permute-start.10 = (bf16[112,2048]{1,0:T(8,128)(2,1)S(1)}, bf16[112,2048]{1,0:T(8,128)(2,1)S(1)}, u32[]{:S(2)}, u32[]{:S(2)}) collective-permute-start(bf16[112,2048]{1,0:T(8,128)(2,1)S(1)} %maximum_convert_fusion), channel_id=1, source_target_pairs={{0,1},{1,0},{2,3},{3,2},{4,5},{5,4},{6,7},{7,6},{8,9},{9,8},{10,11... | collective-permute-start | bytes 1376264 | tf_op jit(solution)/shard_map/ppermute | solution.py:113
  49.3 2.3 %collective-permute-start.4 = (bf16[224,1792]{1,0:T(8,128)(2,1)S(1)}, bf16[224,1792]{1,0:T(8,128)(2,1)S(1)}, u32[]{:S(2)}, u32[]{:S(2)}) collective-permute-start(bf16[224,1792]{1,0:T(8,128)(2,1)S(1)} %pad_maximum_fusion.3), channel_id=1, source_target_pairs={{0,2},{2,0},{4,6},{6,4},{8,10},{10,8},{12,14},{14,12},{16,18},{18,... | collective-permute-start | bytes 2408456 | tf_op jit(solution)/shard_map/ppermute | solution.py:118
  49.3 11.2 %collective-permute-start.11 = (bf16[112,1024]{1,0:T(8,128)(2,1)S(1)}, bf16[112,1024]{1,0:T(8,128)(2,1)S(1)}, u32[]{:S(2)}, u32[]{:S(2)}) collective-permute-start(bf16[112,1024]{1,0:T(8,128)(2,1)S(1)} %slice.228), channel_id=1, source_target_pairs={{0,16},{2,18},{4,20},{6,22},{8,24},{10,26},{12,28},{14,30},{1,17},... | collective-permute-start | bytes 688136 | tf_op jit(solution)/shard_map/ppermute | solution.py:279
  51.9 1.3 collective-permute-start.6
  52.6 7.1 %collective-permute-start.7 = (bf16[56,1792]{1,0:T(8,128)(2,1)S(1)}, bf16[56,1792]{1,0:T(8,128)(2,1)S(1)}, u32[]{:S(2)}, u32[]{:S(2)}) collective-permute-start(bf16[56,1792]{1,0:T(8,128)(2,1)S(1)} %select_convert_fusion.6), channel_id=1, source_target_pairs={{0,4},{2,6},{4,0},{6,2},{8,12},{10,14},{12,8},{14,10},{16,20},{18,... | collective-permute-start | bytes 602120 | tf_op jit(solution)/shard_map/ppermute | solution.py:118
  59.7 9.9 %collective-permute-start.8 = (bf16[56,1792]{1,0:T(8,128)(2,1)S(1)}, bf16[56,1792]{1,0:T(8,128)(2,1)S(1)}, u32[]{:S(2)}, u32[]{:S(2)}) collective-permute-start(bf16[56,1792]{1,0:T(8,128)(2,1)S(1)} %get-tuple-element.212), channel_id=1, source_target_pairs={{0,4},{2,6},{4,0},{6,2},{8,12},{10,14},{12,8},{14,10},{1,5},{3,7},... | collective-permute-start | bytes 602120 | tf_op jit(solution)/shard_map/ppermute | solution.py:118
  60.5 6.0 %copy-start.19 = (bf16[112,1024]{1,0:T(8,128)(2,1)}, bf16[112,1024]{1,0:T(8,128)(2,1)S(1)}, u32[]{:S(2)}) copy-start(bf16[112,1024]{1,0:T(8,128)(2,1)S(1)} %collective-permute-done.11) | copy-start | bytes 688132
  60.5 9.1 %collective-permute-start.9 = (bf16[56,896]{1,0:T(8,128)(2,1)S(1)}, bf16[56,896]{1,0:T(8,128)(2,1)S(1)}, u32[]{:S(2)}, u32[]{:S(2)}) collective-permute-start(bf16[56,896]{1,0:T(8,128)(2,1)S(1)} %select_convert_fusion.9), channel_id=1, source_target_pairs={{0,8},{2,10},{4,12},{6,14},{8,0},{10,2},{12,4},{14,6},{16,24},{18,... | collective-permute-start | bytes 301064 | tf_op jit(solution)/shard_map/ppermute | solution.py:118
  66.5 21.3 %copy-start.4 = (bf16[224,2048]{1,0:T(8,128)(2,1)}, bf16[224,2048]{1,0:T(8,128)(2,1)S(1)}, u32[]{:S(2)}) copy-start(bf16[224,2048]{1,0:T(8,128)(2,1)S(1)} %constant_dynamic-update-slice_fusion.2.refs_1_) | copy-start | bytes 2752516
  71.3 13.5 %collective-permute-start.12 = (bf16[56,1792]{1,0:T(8,128)(2,1)}, bf16[56,1792]{1,0:T(8,128)(2,1)}, u32[]{:S(2)}, u32[]{:S(2)}) collective-permute-start(bf16[56,1792]{1,0:T(8,128)(2,1)} %fusion.7), channel_id=1, source_target_pairs={{0,8},{2,10},{4,12},{6,14},{8,0},{10,2},{12,4},{14,6},{1,9},{3,11}... | collective-permute-start | bytes 602120 | tf_op jit(solution)/shard_map/ppermute | solution.py:118
  73.4 11.4 %collective-permute-start.13 = (bf16[56,896]{1,0:T(8,128)(2,1)}, bf16[56,896]{1,0:T(8,128)(2,1)}, u32[]{:S(2)}, u32[]{:S(2)}) collective-permute-start(bf16[56,896]{1,0:T(8,128)(2,1)} %get-tuple-element.210), channel_id=1, source_target_pairs={{0,16},{2,18},{4,20},{6,22},{8,24},{10,26},{12,28},{14,30},{16,0},... | collective-permute-start | bytes 301064 | tf_op jit(solution)/shard_map/ppermute | solution.py:118
  79.4 8.2 %copy-start.10 = (f32[224,1792]{1,0:T(8,128)S(1)}, f32[224,1792]{1,0:T(8,128)}, u32[]{:S(2)}) copy-start(f32[224,1792]{1,0:T(8,128)} %fusion.29) | copy-start | bytes 4816900
  79.4 8.2 %collective-permute-start.15 = (bf16[112,1024]{1,0:T(8,128)(2,1)}, bf16[112,1024]{1,0:T(8,128)(2,1)S(1)}, u32[]{:S(2)}, u32[]{:S(2)}) collective-permute-start(bf16[112,1024]{1,0:T(8,128)(2,1)} %copy-done.19), channel_id=1, source_target_pairs={{16,17},{17,16},{18,19},{19,18},{20,21},{21,20},{22,23},{23,22},{2... | collective-permute-start | bytes 688136 | tf_op jit(solution)/shard_map/ppermute | solution.py:281
  85.9 5.1 %collective-permute-start.14 = (bf16[56,896]{1,0:T(8,128)(2,1)S(1)}, bf16[56,896]{1,0:T(8,128)(2,1)S(1)}, u32[]{:S(2)}, u32[]{:S(2)}) collective-permute-start(bf16[56,896]{1,0:T(8,128)(2,1)S(1)} %fusion.9), channel_id=1, source_target_pairs={{0,8},{2,10},{4,12},{6,14},{8,0},{10,2},{12,4},{14,6},{16,24},{18,... | collective-permute-start | bytes 301064 | tf_op jit(solution)/shard_map/ppermute | solution.py:118
  87.7 2.1 copy-start.1
  90.9 2.4 %collective-permute-start.17 = (bf16[224,1792]{1,0:T(8,128)(2,1)S(1)}, bf16[224,1792]{1,0:T(8,128)(2,1)S(1)}, u32[]{:S(2)}, u32[]{:S(2)}) collective-permute-start(bf16[224,1792]{1,0:T(8,128)(2,1)S(1)} %pad_maximum_fusion.4), channel_id=1, source_target_pairs={{0,2},{2,0},{4,6},{6,4},{8,10},{10,8},{12,14},{14,12},{16,18},{18,... | collective-permute-start | bytes 2408456 | tf_op jit(solution)/shard_map/ppermute | solution.py:118
  91.1 7.5 %collective-permute-start.16 = (bf16[56,1792]{1,0:T(8,128)(2,1)S(1)}, bf16[56,1792]{1,0:T(8,128)(2,1)S(1)}, u32[]{:S(2)}, u32[]{:S(2)}) collective-permute-start(bf16[56,1792]{1,0:T(8,128)(2,1)S(1)} %pad_maximum_fusion.13), channel_id=1, source_target_pairs={{0,4},{2,6},{4,0},{6,2},{8,12},{10,14},{12,8},{14,10},{16,20},{18,... | collective-permute-start | bytes 602120 | tf_op jit(solution)/shard_map/ppermute | solution.py:118
  98.6 1.5 collective-permute-start.19
  99.3 6.7 %collective-permute-start.20 = (bf16[56,1792]{1,0:T(8,128)(2,1)S(1)}, bf16[56,1792]{1,0:T(8,128)(2,1)S(1)}, u32[]{:S(2)}, u32[]{:S(2)}) collective-permute-start(bf16[56,1792]{1,0:T(8,128)(2,1)S(1)} %select_convert_fusion.4), channel_id=1, source_target_pairs={{0,4},{2,6},{4,0},{6,2},{8,12},{10,14},{12,8},{14,10},{16,20},{18,... | collective-permute-start | bytes 602120 | tf_op jit(solution)/shard_map/ppermute | solution.py:118
  99.9 8.5 %collective-permute-start.18 = (bf16[224,1792]{1,0:T(8,128)(2,1)S(1)}, bf16[224,1792]{1,0:T(8,128)(2,1)S(1)}, u32[]{:S(2)}, u32[]{:S(2)}) collective-permute-start(bf16[224,1792]{1,0:T(8,128)(2,1)S(1)} %pad_maximum_fusion.5), channel_id=1, source_target_pairs={{0,2},{2,0},{4,6},{6,4},{8,10},{10,8},{12,14},{14,12},{16,18},{18,... | collective-permute-start | bytes 2408456 | tf_op jit(solution)/shard_map/ppermute | solution.py:118
  106.0 10.9 %collective-permute-start.23 = (bf16[56,1792]{1,0:T(8,128)(2,1)S(1)}, bf16[56,1792]{1,0:T(8,128)(2,1)S(1)}, u32[]{:S(2)}, u32[]{:S(2)}) collective-permute-start(bf16[56,1792]{1,0:T(8,128)(2,1)S(1)} %get-tuple-element.208), channel_id=1, source_target_pairs={{0,4},{2,6},{4,0},{6,2},{8,12},{10,14},{12,8},{14,10},{1,5},{3,7},... | collective-permute-start | bytes 602120 | tf_op jit(solution)/shard_map/ppermute | solution.py:118
  106.7 10.2 %collective-permute-start.24 = (bf16[56,896]{1,0:T(8,128)(2,1)S(1)}, bf16[56,896]{1,0:T(8,128)(2,1)S(1)}, u32[]{:S(2)}, u32[]{:S(2)}) collective-permute-start(bf16[56,896]{1,0:T(8,128)(2,1)S(1)} %select_convert_fusion.8), channel_id=1, source_target_pairs={{0,8},{2,10},{4,12},{6,14},{8,0},{10,2},{12,4},{14,6},{16,24},{18,... | collective-permute-start | bytes 301064 | tf_op jit(solution)/shard_map/ppermute | solution.py:118
  108.4 4.4 %slice-start.2 = ((s8[7340032]{0:T(1024)(128)(4,1)}), s8[4194304]{0:T(1024)(128)(4,1)S(1)}, s32[]{:S(2)}) async-start(s8[7340032]{0:T(1024)(128)(4,1)} %bitcast.36), calls=%async_computation.2 | async-start | bytes 8388608
  108.5 4.2 %slice-start.3 = ((s8[7340032]{0:T(1024)(128)(4,1)}), s8[3145728]{0:T(1024)(128)(4,1)S(1)}, s32[]{:S(2)}) async-start(s8[7340032]{0:T(1024)(128)(4,1)} %bitcast.36), calls=%async_computation.3 | async-start | bytes 6291456
  109.8 5.3 %copy-start.16 = (f32[224,1024]{1,0:T(8,128)}, f32[224,1024]{1,0:T(8,128)S(1)}, u32[]{:S(2)}) copy-start(f32[224,1024]{1,0:T(8,128)S(1)} %fusion.14) | copy-start | bytes 2752516
  109.8 14.6 %collective-permute-start.22 = (bf16[112,1024]{1,0:T(8,128)(2,1)S(1)}, bf16[112,1024]{1,0:T(8,128)(2,1)S(1)}, u32[]{:S(2)}, u32[]{:S(2)}) collective-permute-start(bf16[112,1024]{1,0:T(8,128)(2,1)S(1)} %slice.329), channel_id=1, source_target_pairs={{16,17},{17,16},{18,19},{19,18},{20,21},{21,20},{22,23},{23,22},{2... | collective-permute-start | bytes 688136 | tf_op jit(solution)/shard_map/ppermute | solution.py:306
  115.4 20.6 %collective-permute-start.21 = (bf16[112,2048]{1,0:T(8,128)(2,1)S(1)}, bf16[112,2048]{1,0:T(8,128)(2,1)S(1)}, u32[]{:S(2)}, u32[]{:S(2)}) collective-permute-start(bf16[112,2048]{1,0:T(8,128)(2,1)S(1)} %fusion.3), channel_id=1, source_target_pairs={{0,1},{1,0},{2,3},{3,2},{4,5},{5,4},{6,7},{7,6},{8,9},{9,8},{10,11... | collective-permute-start | bytes 1376264 | tf_op jit(solution)/shard_map/ppermute | solution.py:113
  118.0 6.5 %slice-start.6 = ((f32[224,1024]{1,0:T(8,128)}), f32[112,1024]{1,0:T(8,128)S(1)}, s32[]{:S(2)}) async-start(f32[224,1024]{1,0:T(8,128)} %copy-done.16), calls=%async_computation.6 | async-start | bytes 917504 | tf_op jit(solution)/shard_map/slice | solution.py:313
  118.0 14.3 %collective-permute-start.26 = (bf16[56,1792]{1,0:T(8,128)(2,1)S(1)}, bf16[56,1792]{1,0:T(8,128)(2,1)S(1)}, u32[]{:S(2)}, u32[]{:S(2)}) collective-permute-start(bf16[56,1792]{1,0:T(8,128)(2,1)S(1)} %fusion.6), channel_id=1, source_target_pairs={{0,8},{2,10},{4,12},{6,14},{8,0},{10,2},{12,4},{14,6},{1,9},{3,11}... | collective-permute-start | bytes 602120 | tf_op jit(solution)/shard_map/ppermute | solution.py:118
  118.8 13.4 %collective-permute-start.27 = (bf16[56,896]{1,0:T(8,128)(2,1)S(1)}, bf16[56,896]{1,0:T(8,128)(2,1)S(1)}, u32[]{:S(2)}, u32[]{:S(2)}) collective-permute-start(bf16[56,896]{1,0:T(8,128)(2,1)S(1)} %get-tuple-element.206), channel_id=1, source_target_pairs={{0,16},{2,18},{4,20},{6,22},{8,24},{10,26},{12,28},{14,30},{16,0},... | collective-permute-start | bytes 301064 | tf_op jit(solution)/shard_map/ppermute | solution.py:118
  124.5 11.5 %collective-permute-start.25 = (bf16[112,1024]{1,0:T(8,128)(2,1)S(1)}, bf16[112,1024]{1,0:T(8,128)(2,1)S(1)}, u32[]{:S(2)}, u32[]{:S(2)}) collective-permute-start(bf16[112,1024]{1,0:T(8,128)(2,1)S(1)} %add_convert_fusion.1), channel_id=1, source_target_pairs={{16,0},{18,2},{20,4},{22,6},{24,8},{26,10},{28,12},{30,14},{17,1},... | collective-permute-start | bytes 688136 | tf_op jit(solution)/shard_map/ppermute | solution.py:315
  133.3 4.7 %collective-permute-start.29 = (bf16[56,896]{1,0:T(8,128)(2,1)S(1)}, bf16[56,896]{1,0:T(8,128)(2,1)S(1)}, u32[]{:S(2)}, u32[]{:S(2)}) collective-permute-start(bf16[56,896]{1,0:T(8,128)(2,1)S(1)} %fusion.8), channel_id=1, source_target_pairs={{0,8},{2,10},{4,12},{6,14},{8,0},{10,2},{12,4},{14,6},{16,24},{18,... | collective-permute-start | bytes 301064 | tf_op jit(solution)/shard_map/ppermute | solution.py:118
  133.4 2.7 %copy-start.14 = (f32[112,2048]{1,0:T(8,128)S(1)}, f32[112,2048]{1,0:T(8,128)}, u32[]{:S(2)}) copy-start(f32[112,2048]{1,0:T(8,128)} %copy-done.13) | copy-start | bytes 2752516
  136.4 11.4 %collective-permute-start.28 = (bf16[112,2048]{1,0:T(8,128)(2,1)S(1)}, bf16[112,2048]{1,0:T(8,128)(2,1)S(1)}, u32[]{:S(2)}, u32[]{:S(2)}) collective-permute-start(bf16[112,2048]{1,0:T(8,128)(2,1)S(1)} %get-tuple-element.171), channel_id=1, source_target_pairs={{0,1},{1,0},{2,3},{3,2},{4,5},{5,4},{6,7},{7,6},{8,9},{9,8},{10,11... | collective-permute-start | bytes 1376264 | tf_op jit(solution)/shard_map/ppermute | solution.py:113
  138.1 9.9 %collective-permute-start.30 = (bf16[56,1792]{1,0:T(8,128)(2,1)S(1)}, bf16[56,1792]{1,0:T(8,128)(2,1)S(1)}, u32[]{:S(2)}, u32[]{:S(2)}) collective-permute-start(bf16[56,1792]{1,0:T(8,128)(2,1)S(1)} %pad_maximum_fusion.14), channel_id=1, source_target_pairs={{0,4},{2,6},{4,0},{6,2},{8,12},{10,14},{12,8},{14,10},{16,20},{18,... | collective-permute-start | bytes 602120 | tf_op jit(solution)/shard_map/ppermute | solution.py:118
  147.9 2.7 %copy-start.8 = (bf16[224,2048]{1,0:T(8,128)(2,1)}, bf16[224,2048]{1,0:T(8,128)(2,1)S(1)}, u32[]{:S(2)}) copy-start(bf16[224,2048]{1,0:T(8,128)(2,1)S(1)} %constant_dynamic-update-slice_fusion.4.refs_2_) | copy-start | bytes 2752516
  148.0 2.4 %collective-permute-start.31 = (bf16[224,1792]{1,0:T(8,128)(2,1)S(1)}, bf16[224,1792]{1,0:T(8,128)(2,1)S(1)}, u32[]{:S(2)}, u32[]{:S(2)}) collective-permute-start(bf16[224,1792]{1,0:T(8,128)(2,1)S(1)} %pad_maximum_fusion.7), channel_id=1, source_target_pairs={{0,2},{2,0},{4,6},{6,4},{8,10},{10,8},{12,14},{14,12},{16,18},{18,... | collective-permute-start | bytes 2408456 | tf_op jit(solution)/shard_map/ppermute | solution.py:118
  152.6 17.6 %collective-permute-start.33 = (bf16[112,1024]{1,0:T(8,128)(2,1)}, bf16[112,1024]{1,0:T(8,128)(2,1)}, u32[]{:S(2)}, u32[]{:S(2)}) collective-permute-start(bf16[112,1024]{1,0:T(8,128)(2,1)} %slice.328), channel_id=1, source_target_pairs={{16,17},{17,16},{18,19},{19,18},{20,21},{21,20},{22,23},{23,22},{2... | collective-permute-start | bytes 688136 | tf_op jit(solution)/shard_map/ppermute | solution.py:306
  158.5 3.3 %copy-start.6 = (bf16[1024,1792]{1,0:T(8,128)(2,1)S(1)}, bf16[1024,1792]{1,0:T(8,128)(2,1)}, u32[]{:S(2)}) copy-start(bf16[1024,1792]{1,0:T(8,128)(2,1)} %refs_5_.4) | copy-start | bytes 11010052
  158.5 3.8 %copy-start.7 = (bf16[1024,1792]{1,0:T(8,128)(2,1)S(1)}, bf16[1024,1792]{1,0:T(8,128)(2,1)}, u32[]{:S(2)}) copy-start(bf16[1024,1792]{1,0:T(8,128)(2,1)} %refs_6_.4) | copy-start | bytes 11010052
  161.3 25.6 %collective-permute-start.32 = (bf16[112,2048]{1,0:T(8,128)(2,1)}, bf16[112,2048]{1,0:T(8,128)(2,1)}, u32[]{:S(2)}, u32[]{:S(2)}) collective-permute-start(bf16[112,2048]{1,0:T(8,128)(2,1)} %fusion.2), channel_id=1, source_target_pairs={{0,1},{1,0},{2,3},{3,2},{4,5},{5,4},{6,7},{7,6},{8,9},{9,8},{10,11... | collective-permute-start | bytes 1376264 | tf_op jit(solution)/shard_map/ppermute | solution.py:113
  170.2 6.3 %copy-start.3 = (bf16[224,2048]{1,0:T(8,128)(2,1)S(1)}, bf16[224,2048]{1,0:T(8,128)(2,1)}, u32[]{:S(2)}) copy-start(bf16[224,2048]{1,0:T(8,128)(2,1)} %copy-done.2) | copy-start | bytes 2752516
  170.2 6.3 %copy-start.5 = (bf16[224,2048]{1,0:T(8,128)(2,1)S(1)}, bf16[224,2048]{1,0:T(8,128)(2,1)}, u32[]{:S(2)}) copy-start(bf16[224,2048]{1,0:T(8,128)(2,1)} %copy-done.4) | copy-start | bytes 2752516
  171.5 15.4 %collective-permute-start.34 = (bf16[112,1024]{1,0:T(8,128)(2,1)S(1)}, bf16[112,1024]{1,0:T(8,128)(2,1)S(1)}, u32[]{:S(2)}, u32[]{:S(2)}) collective-permute-start(bf16[112,1024]{1,0:T(8,128)(2,1)S(1)} %add_convert_fusion), channel_id=1, source_target_pairs={{16,0},{18,2},{20,4},{22,6},{24,8},{26,10},{28,12},{30,14},{17,1},... | collective-permute-start | bytes 688136 | tf_op jit(solution)/shard_map/ppermute | solution.py:315
  186.9 1.4 copy-start.18
  188.6 13.7 %collective-permute-start.35 = (bf16[112,2048]{1,0:T(8,128)(2,1)S(1)}, bf16[112,2048]{1,0:T(8,128)(2,1)S(1)}, u32[]{:S(2)}, u32[]{:S(2)}) collective-permute-start(bf16[112,2048]{1,0:T(8,128)(2,1)S(1)} %get-tuple-element.197), channel_id=1, source_target_pairs={{0,1},{1,0},{2,3},{3,2},{4,5},{5,4},{6,7},{7,6},{8,9},{9,8},{10,11... | collective-permute-start | bytes 1376264 | tf_op jit(solution)/shard_map/ppermute | solution.py:113
  189.6 12.7 %slice-start.4 = ((s8[7340032]{0:T(1024)(128)(4,1)}), s8[4194304]{0:T(1024)(128)(4,1)S(1)}, s32[]{:S(2)}) async-start(s8[7340032]{0:T(1024)(128)(4,1)} %bitcast.38), calls=%async_computation.4 | async-start | bytes 8388608
  189.6 12.0 %copy-start.22 = (bf16[2048]{0:T(1024)(128)(2,1)S(1)}, bf16[2048]{0:T(1024)(128)(2,1)}, u32[]{:S(2)}) copy-start(bf16[2048]{0:T(1024)(128)(2,1)} %param.23) | copy-start | bytes 12292
  189.6 12.0 %copy-start.23 = (bf16[2048]{0:T(1024)(128)(2,1)S(1)}, bf16[2048]{0:T(1024)(128)(2,1)}, u32[]{:S(2)}) copy-start(bf16[2048]{0:T(1024)(128)(2,1)} %param.22) | copy-start | bytes 12292
  189.6 12.7 %slice-start.5 = ((s8[7340032]{0:T(1024)(128)(4,1)}), s8[3145728]{0:T(1024)(128)(4,1)S(1)}, s32[]{:S(2)}) async-start(s8[7340032]{0:T(1024)(128)(4,1)} %bitcast.38), calls=%async_computation.5 | async-start | bytes 6291456
  189.6 11.9 %collective-permute-start.36 = (f32[2048]{0:T(1024)S(1)}, f32[2048]{0:T(1024)S(1)}, u32[]{:S(2)}, u32[]{:S(2)}) collective-permute-start(f32[2048]{0:T(1024)S(1)} %add.230), channel_id=1, source_target_pairs={{0,1},{1,0},{2,3},{3,2},{4,5},{5,4},{6,7},{7,6},{8,9},{9,8},{10,11... | collective-permute-start | bytes 24584 | tf_op jit(solution)/shard_map/ppermute | solution.py:113
  (4 other events, 4.4 us)
